TPU v7x, 32 devices: a whole 2x2x4 slice. The times are simulated.
32 devices in a mesh: fsdp: 8 (over z, x), seq: 4 (over y, core).
Axes of the slice: x: 2, y: 2, z: 4, core: 2. Of those that a mesh axis runs over, the one named last changes fastest.
Arguments:
- tokens: bfloat16 [8, 512, 768], P('fsdp', 'seq'), may hold values from -6 to 6
- encoder: bfloat16 [8, 512, 768], P('fsdp'), may hold values from -6 to 6
- dec_segments: int32 [8, 512], P('fsdp'), may hold values from 0 to 2, never falling along the last dimension, each value on 1 to 320 neighbouring positions
- enc_segments: int32 [8, 512], P('fsdp'), may hold values from 0 to 2, never falling along the last dimension, each value on 1 to 320 neighbouring positions
- buckets: int32 [512], replicated, may hold values from 0 to 31, as said below
- self_gain: bfloat16 [768], P(('fsdp', 'seq')), may hold values from 0.5 to 1.5
- self_query: bfloat16 [589824], P(('fsdp', 'seq')), may hold values from -0.0546875 to 0.0546875
- self_key: bfloat16 [589824], P(('fsdp', 'seq')), may hold values from -0.21875 to 0.21875
- self_value: bfloat16 [589824], P(('fsdp', 'seq')), may hold values from -0.21875 to 0.21875
- self_output: bfloat16 [589824], P(('fsdp', 'seq')), may hold values from -0.625 to 0.625
- bias_table: bfloat16 [32, 12], replicated, may hold values from -4 to 4
- cross_gain: bfloat16 [768], P(('fsdp', 'seq')), may hold values from 0.5 to 1.5
- cross_query: bfloat16 [589824], P(('fsdp', 'seq')), may hold values from -0.0546875 to 0.0546875
- cross_key: bfloat16 [589824], P(('fsdp', 'seq')), may hold values from -0.21875 to 0.21875
- cross_value: bfloat16 [589824], P(('fsdp', 'seq')), may hold values from -0.21875 to 0.21875
- cross_output: bfloat16 [589824], P(('fsdp', 'seq')), may hold values from -0.625 to 0.625
- ffn_gain: bfloat16 [768], P(('fsdp', 'seq')), may hold values from 0.5 to 1.5
- ffn_gate: bfloat16 [1572864], P(('fsdp', 'seq')), may hold values from -0.21875 to 0.21875
- ffn_up: bfloat16 [1572864], P(('fsdp', 'seq')), may hold values from -0.21875 to 0.21875
- ffn_down: bfloat16 [1572864], P(('fsdp', 'seq')), may hold values from -0.25 to 0.25
- cotangent: bfloat16 [8, 512, 768], P('fsdp', 'seq'), may hold values from -6 to 6
Outputs:
- output: bfloat16 [8, 512, 768], P('fsdp', 'seq')
- grad_tokens: float32 [8, 512, 768], P('fsdp', 'seq')
- grad_encoder: float32 [8, 512, 768], P('fsdp', 'seq')
- grad_self_gain: float32 [768], P(('fsdp', 'seq'))
- grad_self_query: float32 [589824], P(('fsdp', 'seq'))
- grad_self_key: float32 [589824], P(('fsdp', 'seq'))
- grad_self_value: float32 [589824], P(('fsdp', 'seq'))
- grad_self_output: float32 [589824], P(('fsdp', 'seq'))
- grad_bias_table: float32 [32, 12], replicated
- grad_cross_gain: float32 [768], P(('fsdp', 'seq'))
- grad_cross_query: float32 [589824], P(('fsdp', 'seq'))
- grad_cross_key: float32 [589824], P(('fsdp', 'seq'))
- grad_cross_value: float32 [589824], P(('fsdp', 'seq'))
- grad_cross_output: float32 [589824], P(('fsdp', 'seq'))
- grad_ffn_gain: float32 [768], P(('fsdp', 'seq'))
- grad_ffn_gate: float32 [1572864], P(('fsdp', 'seq'))
- grad_ffn_up: float32 [1572864], P(('fsdp', 'seq'))
- grad_ffn_down: float32 [1572864], P(('fsdp', 'seq'))
Inputs may be any that keep to these rules, and one draw needn't show every extreme that they name: buckets[d] is the bucket of a key d positions before its query; it never falls as d grows, equals d for d below 16, and its last entry is 31. `dec_segments`: along each row the ids never fall; every id 0 to 2 appears; the longest document has 320 positions. `enc_segments`: along each row the ids never fall; every id 0 to 2 appears, so each decoder document has encoder positions in its row; the longest has 320 positions.
All inputs are finite; a program needn't handle non-finite values.
Results may differ from a plain program's by a relative error of at most 0.023.
The roundings to bfloat16 on the way count: a program that leaves them out, or rounds other values in their place, can miss the bound.
Values may be sent and summed in bfloat16 or wider, within the bound.
A program may use at most 256 MiB of HBM per device.

v0:
```python
import jax
import jax.numpy as jnp
from jax import lax
from jax.sharding import PartitionSpec as P

HEADS = 12
HEAD_DIM = 64
epsilon = 1e-06
masked_value = -1e30
highest = lax.Precision.HIGHEST


def matmul(first_op, second_op):
    return jnp.dot(first_op, second_op, preferred_element_type=jnp.float32)


def contract_rows(first_op, second_op):
    return lax.dot_general(
        first_op, second_op, (((0,), (0,)), ((), ())), preferred_element_type=jnp.float32
    )


def times_transposed(first_op, second_op):
    return lax.dot_general(
        first_op, second_op, (((1,), (1,)), ((), ())), preferred_element_type=jnp.float32
    )


def rms_forward(values, gain_vector):
    factor = lax.rsqrt(jnp.mean(values * values, axis=-1, keepdims=True) + epsilon)
    return ((values * factor * gain_vector.astype(jnp.float32)).astype(jnp.bfloat16), factor)


def rms_backward(values, factor, gain_vector, upstream):
    scaled = upstream * gain_vector.astype(jnp.float32)
    inner_mean = jnp.mean(scaled * values, axis=-1, keepdims=True)
    grad_values = factor * scaled - values * (factor * factor * factor) * inner_mean
    grad_gain = jnp.sum(upstream * values * factor, axis=0)
    return (grad_values, grad_gain)


def gather_rows(packed):
    return lax.all_gather(packed, ("fsdp", "seq"), axis=0, tiled=True)


def scatter_rows(partial):
    return lax.psum_scatter(partial, ("fsdp", "seq"), scatter_dimension=0, tiled=True)


def scatter_to_owner(partial, row_count, block):
    count = lax.axis_size("seq")
    index = lax.axis_index("seq")
    total = lax.dynamic_slice_in_dim(partial, index * block, block, 1).astype(jnp.float32)
    for step in range(1, count):
        target = lax.rem(index + step, count)
        piece = lax.dynamic_slice_in_dim(partial, target * block, block, 1)
        pairs = [(source, (source + step) % count) for source in range(count)]
        total = total + lax.ppermute(piece, "seq", pairs).astype(jnp.float32)
    return total.astype(jnp.bfloat16)


def sum_everywhere(values):
    for axis in ("seq", "fsdp"):
        count = lax.axis_size(axis)
        step = 1
        while step < count:
            pairs = [(source, source ^ step) for source in range(count)]
            values = values + lax.ppermute(values, axis, pairs)
            step *= 2
    return values


def split_heads(values, row_count):
    return values.reshape(row_count, -1, HEADS, HEAD_DIM)


def score_block(query_heads, key_heads, position_bias, allowed):
    scores = (
        jnp.einsum("rqhd,rkhd->rhqk", query_heads, key_heads, preferred_element_type=jnp.float32)
        + position_bias
    )
    return jnp.where(allowed[:, None], scores, masked_value)


def attend(query_heads, key_heads, value_heads, position_bias, allowed):
    scores = score_block(query_heads, key_heads, position_bias, allowed)
    maximum = jnp.max(scores, axis=-1, keepdims=True)
    log_total = maximum + jnp.log(jnp.sum(jnp.exp(scores - maximum), axis=-1, keepdims=True))
    attn_probs = jnp.exp(scores - log_total).astype(jnp.bfloat16)
    mixed_heads = jnp.einsum(
        "rhqk,rkhd->rqhd", attn_probs, value_heads, preferred_element_type=jnp.float32
    )
    return (mixed_heads.astype(jnp.bfloat16), log_total)


def attend_back(query_heads, key_heads, value_heads, position_bias, allowed, log_total, grad_mixed):
    scores = score_block(query_heads, key_heads, position_bias, allowed)
    attn_probs = jnp.exp(scores - log_total)
    grad_probs = jnp.einsum(
        "rqhd,rkhd->rhqk", grad_mixed, value_heads, preferred_element_type=jnp.float32
    )
    grad_value = jnp.einsum(
        "rhqk,rqhd->rkhd",
        attn_probs.astype(jnp.bfloat16),
        grad_mixed,
        preferred_element_type=jnp.float32,
    )
    row_sums = jnp.sum(attn_probs * grad_probs, axis=-1, keepdims=True)
    grad_scores = attn_probs * (grad_probs - row_sums)
    low_scores = grad_scores.astype(jnp.bfloat16)
    grad_query = jnp.einsum(
        "rhqk,rkhd->rqhd", low_scores, key_heads, preferred_element_type=jnp.float32
    ).astype(jnp.bfloat16)
    grad_key = jnp.einsum(
        "rhqk,rqhd->rkhd", low_scores, query_heads, preferred_element_type=jnp.float32
    )
    return (grad_scores, grad_query, grad_key, grad_value)


def geglu(gate_part, up_part):
    return jax.nn.gelu(gate_part, approximate=True) * up_part


def per_device(
    tokens,
    encoder,
    dec_segments,
    enc_segments,
    buckets,
    self_gain,
    self_query,
    self_key,
    self_value,
    self_output,
    bias_table,
    cross_gain,
    cross_query,
    cross_key,
    cross_value,
    cross_output,
    ffn_gain,
    ffn_gate,
    ffn_up,
    ffn_down,
    cotangent,
):
    row_count, block_len, model_width = tokens.shape
    full_len = dec_segments.shape[1]
    enc_len = encoder.shape[1]
    seq_count = lax.axis_size("seq")
    seq_index = lax.axis_index("seq")
    enc_block = enc_len // seq_count
    inputs_flat = tokens.reshape(row_count * block_len, model_width).astype(jnp.float32)
    query_pos = seq_index * block_len + jnp.arange(block_len, dtype=jnp.int32)
    key_pos = jnp.arange(full_len, dtype=jnp.int32)
    distance = query_pos[:, None] - key_pos[None, :]
    bucket_ids = jnp.arange(bias_table.shape[0], dtype=jnp.int32)
    first = jnp.sum((buckets[None, :] < bucket_ids[:, None]).astype(jnp.int32), axis=1)
    beyond = jnp.sum((buckets[None, :] <= bucket_ids[:, None]).astype(jnp.int32), axis=1)
    clipped = jnp.clip(distance, 0, full_len - 1)[:, None, :]
    onehot = ((clipped >= first[None, :, None]) & (clipped < beyond[None, :, None])).astype(
        jnp.bfloat16
    )
    position_bias = jnp.einsum(
        "qbk,bh->hqk", onehot, bias_table, preferred_element_type=jnp.float32
    )
    own_segments = lax.dynamic_slice_in_dim(dec_segments, seq_index * block_len, block_len, 1)
    self_allowed = (distance >= 0)[None] & (own_segments[:, :, None] == dec_segments[:, None, :])
    cross_allowed = own_segments[:, :, None] == enc_segments[:, None, :]
    own_rows = self_gain.shape[0]
    gains = jnp.pad(jnp.stack([self_gain, cross_gain, ffn_gain], axis=1), ((0, 0), (0, 125)))

    def rows_of(flat):
        return flat.reshape(own_rows, -1)

    packed_self = gather_rows(
        jnp.concatenate(
            [rows_of(w) for w in (self_query, self_key, self_value, self_output)] + [gains], axis=1
        )
    )
    packed_rest = gather_rows(
        jnp.concatenate(
            [
                rows_of(w)
                for w in (cross_query, cross_key, cross_value, cross_output, ffn_gate, ffn_up)
            ],
            axis=1,
        )
    )
    packed_cross = packed_rest[:, : 4 * model_width]
    packed_in = packed_rest[:, 4 * model_width :]
    packed_down = gather_rows(ffn_down.reshape(-1, model_width))
    all_gains = packed_self[:, 4 * model_width :]

    def columns(packed, index):
        return packed[:, index * model_width : (index + 1) * model_width]

    hidden_width = packed_down.shape[0]
    self_full = [all_gains[:, 0]] + [columns(packed_self, index) for index in range(4)]
    cross_full = [all_gains[:, 1]] + [columns(packed_cross, index) for index in range(4)]
    ffn_full = [
        all_gains[:, 2],
        packed_in[:, :hidden_width],
        packed_in[:, hidden_width:],
        packed_down,
    ]
    norm_one, factor_one = rms_forward(inputs_flat, self_full[0])
    qkv_one = matmul(norm_one, packed_self[:, : 3 * model_width]).astype(jnp.bfloat16)
    query_one = qkv_one[:, :model_width]
    pair_all = lax.all_gather(
        qkv_one[:, model_width:].reshape(row_count, block_len, 2 * model_width),
        "seq",
        axis=1,
        tiled=True,
    )
    key_all = pair_all[:, :, :model_width]
    value_all = pair_all[:, :, model_width:]
    query_heads_one = split_heads(query_one, row_count)
    key_heads_one = split_heads(key_all, row_count)
    value_heads_one = split_heads(value_all, row_count)
    mixed_one, lse_one = attend(
        query_heads_one, key_heads_one, value_heads_one, position_bias[None], self_allowed
    )
    mixed_one = mixed_one.reshape(row_count * block_len, model_width)
    hidden_one = inputs_flat + matmul(mixed_one, self_full[4])
    norm_two, factor_two = rms_forward(hidden_one, cross_full[0])
    query_two = matmul(norm_two, cross_full[1]).astype(jnp.bfloat16)
    enc_own = lax.dynamic_slice_in_dim(encoder, seq_index * enc_block, enc_block, 1).reshape(
        row_count * enc_block, model_width
    )
    enc_flat = encoder.reshape(row_count * enc_len, model_width)
    key_two = matmul(enc_flat, cross_full[2]).astype(jnp.bfloat16)
    value_two = matmul(enc_flat, cross_full[3]).astype(jnp.bfloat16)
    query_heads_two = split_heads(query_two, row_count)
    key_heads_two = split_heads(key_two, row_count)
    value_heads_two = split_heads(value_two, row_count)
    mixed_two, lse_two = attend(query_heads_two, key_heads_two, value_heads_two, 0.0, cross_allowed)
    mixed_two = mixed_two.reshape(row_count * block_len, model_width)
    hidden_two = hidden_one + matmul(mixed_two, cross_full[4])
    norm_three, factor_three = rms_forward(hidden_two, ffn_full[0])
    gate_value = matmul(norm_three, ffn_full[1])
    up_value = matmul(norm_three, ffn_full[2])
    activation, geglu_back = jax.vjp(geglu, gate_value, up_value)
    hidden_act = activation.astype(jnp.bfloat16)
    result = hidden_two + matmul(hidden_act, ffn_full[3])
    output = result.astype(jnp.bfloat16).reshape(row_count, block_len, model_width)
    self_back = self_full
    cross_back = cross_full
    ffn_back = ffn_full
    grad_out = cotangent.reshape(row_count * block_len, model_width).astype(jnp.float32)
    low_out = grad_out.astype(jnp.bfloat16)
    grad_down = contract_rows(hidden_act, low_out)
    grad_hidden = times_transposed(low_out, ffn_back[3])
    grad_gate, grad_up = geglu_back(grad_hidden)
    low_gate = grad_gate.astype(jnp.bfloat16)
    low_up = grad_up.astype(jnp.bfloat16)
    low_in = jnp.concatenate([low_gate, low_up], axis=1)
    summed_in = scatter_rows(contract_rows(norm_three, low_in).astype(jnp.bfloat16))
    summed_down = scatter_rows(grad_down.astype(jnp.bfloat16))
    grad_norm_three = times_transposed(low_in, packed_in)
    grad_residual_three, grad_gain_three = rms_backward(
        hidden_two, factor_three, ffn_back[0], grad_norm_three
    )
    grad_two = grad_out + grad_residual_three
    low_two = grad_two.astype(jnp.bfloat16)
    grad_cross_out = contract_rows(mixed_two, low_two)
    grad_mixed_two = times_transposed(low_two, cross_back[4]).astype(jnp.bfloat16)
    unused_scores, grad_query_two, grad_key_part_two, grad_value_part_two = attend_back(
        query_heads_two,
        key_heads_two,
        value_heads_two,
        0.0,
        cross_allowed,
        lse_two,
        split_heads(grad_mixed_two, row_count),
    )
    pair_two = jnp.concatenate(
        [
            grad_key_part_two.reshape(row_count, enc_len, model_width),
            grad_value_part_two.reshape(row_count, enc_len, model_width),
        ],
        axis=2,
    ).astype(jnp.bfloat16)
    low_pair_two = scatter_to_owner(pair_two, row_count, enc_block).reshape(
        row_count * enc_block, 2 * model_width
    )
    grad_cross_pair = contract_rows(enc_own, low_pair_two)
    grad_encoder = times_transposed(
        low_pair_two, packed_cross[:, model_width : 3 * model_width]
    ).reshape(row_count, enc_block, model_width)
    low_query_two = grad_query_two.reshape(row_count * block_len, model_width)
    grad_cross_query = contract_rows(norm_two, low_query_two)
    grad_norm_two = times_transposed(low_query_two, cross_back[1])
    summed_cross = scatter_rows(
        jnp.concatenate([grad_cross_query, grad_cross_pair, grad_cross_out], axis=1).astype(
            jnp.bfloat16
        )
    )
    grad_residual_two, grad_gain_two = rms_backward(
        hidden_one, factor_two, cross_back[0], grad_norm_two
    )
    grad_one = grad_two + grad_residual_two
    low_one = grad_one.astype(jnp.bfloat16)
    grad_self_out = contract_rows(mixed_one, low_one)
    grad_mixed_one = times_transposed(low_one, self_back[4]).astype(jnp.bfloat16)
    grad_scores_one, grad_query_one, grad_key_part_one, grad_value_part_one = attend_back(
        query_heads_one,
        key_heads_one,
        value_heads_one,
        position_bias[None],
        self_allowed,
        lse_one,
        split_heads(grad_mixed_one, row_count),
    )
    grad_table = jnp.einsum(
        "qbk,rhqk->bh", onehot.astype(jnp.float32), grad_scores_one, precision=highest
    )
    pair_one = jnp.concatenate(
        [
            grad_key_part_one.reshape(row_count, full_len, model_width),
            grad_value_part_one.reshape(row_count, full_len, model_width),
        ],
        axis=2,
    ).astype(jnp.bfloat16)
    low_pair_one = scatter_to_owner(pair_one, row_count, block_len).reshape(
        row_count * block_len, 2 * model_width
    )
    low_query_one = grad_query_one.reshape(row_count * block_len, model_width)
    low_qkv_one = jnp.concatenate([low_query_one, low_pair_one], axis=1)
    grad_self_qkv = contract_rows(norm_one, low_qkv_one)
    grad_norm_one = times_transposed(low_qkv_one, packed_self[:, : 3 * model_width])
    grad_residual_one, grad_gain_one = rms_backward(
        inputs_flat, factor_one, self_back[0], grad_norm_one
    )
    grad_tokens = (grad_one + grad_residual_one).reshape(row_count, block_len, model_width)
    summed_self = scatter_rows(
        jnp.concatenate([grad_self_qkv, grad_self_out], axis=1).astype(jnp.bfloat16)
    )
    table_items = grad_table.size
    small_parts = jnp.concatenate(
        [grad_table.reshape(-1), grad_gain_one, grad_gain_two, grad_gain_three]
    )
    small_sum = sum_everywhere(small_parts.reshape(-1, 128)).reshape(-1)
    table_grad = small_sum[:table_items].reshape(grad_table.shape)
    own_index = lax.axis_index("fsdp") * seq_count + seq_index

    def flat_columns(summed, start, width):
        return summed[:, start : start + width].reshape(-1).astype(jnp.float32)

    def gain_grad(index):
        start = table_items + index * model_width + own_index * own_rows
        return lax.dynamic_slice_in_dim(small_sum, start, own_rows, 0)

    return (
        output,
        grad_tokens,
        grad_encoder,
        gain_grad(0),
        *[flat_columns(summed_self, index * model_width, model_width) for index in range(4)],
        table_grad,
        gain_grad(1),
        *[flat_columns(summed_cross, index * model_width, model_width) for index in range(4)],
        gain_grad(2),
        flat_columns(summed_in, 0, hidden_width),
        flat_columns(summed_in, hidden_width, hidden_width),
        summed_down.reshape(-1).astype(jnp.float32),
    )


def solution(mesh):
    in_specs = (
        P("fsdp", "seq", None),
        P("fsdp", None, None),
        P("fsdp", None),
        P("fsdp", None),
        P(),
        P(("fsdp", "seq")),
        P(("fsdp", "seq")),
        P(("fsdp", "seq")),
        P(("fsdp", "seq")),
        P(("fsdp", "seq")),
        P(),
        P(("fsdp", "seq")),
        P(("fsdp", "seq")),
        P(("fsdp", "seq")),
        P(("fsdp", "seq")),
        P(("fsdp", "seq")),
        P(("fsdp", "seq")),
        P(("fsdp", "seq")),
        P(("fsdp", "seq")),
        P(("fsdp", "seq")),
        P("fsdp", "seq", None),
    )
    out_specs = (
        P("fsdp", "seq", None),
        P("fsdp", "seq", None),
        P("fsdp", "seq", None),
        P(("fsdp", "seq")),
        P(("fsdp", "seq")),
        P(("fsdp", "seq")),
        P(("fsdp", "seq")),
        P(("fsdp", "seq")),
        P(),
        P(("fsdp", "seq")),
        P(("fsdp", "seq")),
        P(("fsdp", "seq")),
        P(("fsdp", "seq")),
        P(("fsdp", "seq")),
        P(("fsdp", "seq")),
        P(("fsdp", "seq")),
        P(("fsdp", "seq")),
        P(("fsdp", "seq")),
    )
    return jax.shard_map(
        per_device, mesh=mesh, in_specs=in_specs, out_specs=out_specs, check_vma=False
    )
```

profile of v0, /device:TPU:0, one launch (start us, length us, event | category | flops | bytes accessed | tf_op | source)
XLA Modules:
  0.0 729.4 jit_solution(9494032237790957650)
XLA Ops:
  12.2 1.6 reshape.634
  15.5 63.9 %all-gather.6.cloned.1.call-done = bf16[768,3200]{1,0:T(8,128)(2,1)} async-done(((bf16[24,3200]{1,0:T(8,128)(2,1)}), bf16[768,3200]{1,0:T(8,128)(2,1)}) %all-gather.6.cloned.1.call-update) | async-done | bytes 4915216 | tf_op jit(solution)/shard_map/all_gather | solution.py:43
  79.4 2.1 convert_reduce_fusion
  81.5 2.9 convolution_convert_fusion.2
  87.6 3.9 fusion.1
  91.5 5.5 copy.111
  97.3 43.5 %all-gather.10.cloned.1.call-done = bf16[2048,768]{1,0:T(8,128)(2,1)} async-done(((bf16[64,768]{1,0:T(8,128)(2,1)}), bf16[2048,768]{1,0:T(8,128)(2,1)}) %all-gather.10.cloned.1.call-update) | async-done | bytes 3145744 | tf_op jit(solution)/shard_map/all_gather | solution.py:43
  140.7 4.0 fusion.75
  145.0 16.4 %all-gather.12.cloned.1.call-done = bf16[512,1536]{1,0:T(8,128)(2,1)} async-done(((bf16[128,1536]{1,0:T(8,128)(2,1)}), bf16[512,1536]{1,0:T(8,128)(2,1)}) %all-gather.12.cloned.1.call-update) | async-done | bytes 1572880 | tf_op jit(solution)/shard_map/all_gather | solution.py:210
  163.5 2.9 fusion.97
  168.2 1.8 multiply_reduce_fusion.7
  170.6 82.5 %all-gather.8.cloned.1.call-done = bf16[768,7168]{1,0:T(8,128)(2,1)} async-done(((bf16[24,7168]{1,0:T(8,128)(2,1)}), bf16[768,7168]{1,0:T(8,128)(2,1)}) %all-gather.8.cloned.1.call-update) | async-done | bytes 11010064 | tf_op jit(solution)/shard_map/all_gather | solution.py:43
  253.1 1.6 convolution_convert_fusion.19
  254.9 2.2 convolution_convert_fusion.8
  258.9 2.0 copy-done.23
  266.0 2.8 multiply_reduce_fusion.2
  268.8 2.8 convolution_convert_fusion.4
  271.9 1.9 convolution_convert_fusion.17
  274.1 3.6 multiply_reduce_fusion.1
  285.4 1.6 convolution_convert_fusion.5
  287.0 2.4 copy.119
  292.1 1.7 collective-permute-done.4
  293.7 6.6 collective-permute-done.5
  302.6 2.6 pad_maximum_fusion.1
  305.2 2.8 multiply_reduce_fusion.3
  310.1 2.5 convolution_convert_fusion.15
  312.6 1.7 copy.114
  314.3 2.3 multiply_reduce_fusion
  320.6 1.5 collective-permute-start.1
  323.5 10.8 %collective-permute-done = bf16[1,128,1536]{1,2,0:T(8,128)(2,1)S(1)} collective-permute-done((bf16[1,128,1536]{1,2,0:T(8,128)(2,1)S(1)}, bf16[1,128,1536]{1,2,0:T(8,128)(2,1)S(1)}, u32[]{:S(2)}, u32[]{:S(2)}) %collective-permute-start) | collective-permute-done | bytes 393248 | tf_op jit(solution)/shard_map/ppermute | solution.py:58
  335.1 5.9 collective-permute-done.2
  342.4 2.8 pad_maximum_fusion
  346.6 4.5 convolution_convert_fusion
  351.1 1.9 copy-done.7
  352.9 3.5 copy.115
  356.5 6.5 fusion.29
  363.7 5.0 fusion.61
  369.9 2.0 collective-permute-start.6
  374.2 2.3 fusion.28
  377.6 1.5 collective-permute-start.8
  379.1 3.4 fusion.22
  382.5 1.5 collective-permute-start.9
  384.0 2.2 collective-permute-done.9
  386.2 2.4 collective-permute-start.10
  392.2 1.7 reshape.664
  393.9 94.4 %reduce-scatter.7.cloned.1.call-done = bf16[24,3072]{1,0:T(8,128)(2,1)} async-done(((bf16[768,3072]{1,0:T(8,128)(2,1)}), bf16[24,3072]{1,0:T(8,128)(2,1)}) %reduce-scatter.7.cloned.1.call-update) | async-done | bytes 147472 | tf_op jit(solution)/shard_map/reduce_scatter | solution.py:47
  491.6 109.0 %reduce-scatter.5.cloned.1.call-done = bf16[24,3072]{1,0:T(8,128)(2,1)} async-done(((bf16[768,3072]{1,0:T(8,128)(2,1)}), bf16[24,3072]{1,0:T(8,128)(2,1)}) %reduce-scatter.5.cloned.1.call-update) | async-done | bytes 147472 | tf_op jit(solution)/shard_map/reduce_scatter | solution.py:47
  604.1 115.9 %reduce-scatter.9.cloned.1.call-done = bf16[24,4096]{1,0:T(8,128)(2,1)} async-done(((bf16[768,4096]{1,0:T(8,128)(2,1)}), bf16[24,4096]{1,0:T(8,128)(2,1)}) %reduce-scatter.9.cloned.1.call-update) | async-done | bytes 196624 | tf_op jit(solution)/shard_map/reduce_scatter | solution.py:47
  (316 shorter events, 62.8 us)
Async XLA Ops:
  7.2 247.7 %copy-start = (bf16[1,512,768]{2,1,0:T(8,128)(2,1)S(1)}, bf16[1,512,768]{2,1,0:T(8,128)(2,1)}, u32[]{:S(2)}) copy-start(bf16[1,512,768]{2,1,0:T(8,128)(2,1)} %param.22) | copy-start | bytes 2359300
  7.2 72.2 %all-gather.6.cloned.1.call-start = ((), (), s32[]{:S(2)}) async-start(), calls=%async_computation.4 | async-start | bytes 5068800 | tf_op jit(solution)/shard_map/all_gather | solution.py:43
  12.2 128.6 %all-gather.10.cloned.1.call-start = ((), (), s32[]{:S(2)}) async-start(), calls=%async_computation.6 | async-start | bytes 3244032 | tf_op jit(solution)/shard_map/all_gather | solution.py:43
  13.9 147.5 %all-gather.12.cloned.1.call-start = ((), (), s32[]{:S(2)}) async-start(), calls=%async_computation.11 | async-start | bytes 1966080 | tf_op jit(solution)/shard_map/all_gather | solution.py:210
  15.5 69.7 %copy-start.84 = (f32[128]{0:T(128)}, f32[128]{0:T(128)S(1)}, u32[]{:S(2)}) copy-start(f32[128]{0:T(128)S(1)} %get-tuple-element.126) | copy-start | bytes 1540
  81.5 171.6 %copy-start.59 = (f32[768]{0:T(1024)}, f32[768]{0:T(1024)S(1)}, u32[]{:S(2)}) copy-start(f32[768]{0:T(1024)S(1)} %get-tuple-element.91) | copy-start | bytes 9220
  85.2 167.8 %all-gather.8.cloned.1.call-start = ((), (), s32[]{:S(2)}) async-start(), calls=%async_computation.5 | async-start | bytes 11354112 | tf_op jit(solution)/shard_map/all_gather | solution.py:43
  86.5 305.7 %reduce-scatter.11.cloned.1.call-start = ((), (), s32[]{:S(2)}) async-start(), calls=%async_computation.10 | async-start | bytes 3244032 | tf_op jit(solution)/shard_map/reduce_scatter | solution.py:47
  86.9 10.1 %copy-start.55 = (s32[128,512]{0,1:T(8,128)}, s32[128,512]{0,1:T(8,128)S(1)}, u32[]{:S(2)}) copy-start(s32[128,512]{0,1:T(8,128)S(1)} %copy.110) | copy-start | bytes 786436
  91.5 49.2 %copy-start.39 = (bf16[1,128,768]{2,1,0:T(8,128)(2,1)S(1)}, bf16[1,128,768]{2,1,0:T(8,128)(2,1)}, u32[]{:S(2)}) copy-start(bf16[1,128,768]{2,1,0:T(8,128)(2,1)} %param.41) | copy-start | bytes 589828
  97.3 164.5 %copy-start.24 = (pred[128,512]{1,0:T(8,128)(4,1)}, pred[128,512]{1,0:T(8,128)(4,1)S(1)}, u32[]{:S(2)}) copy-start(pred[128,512]{1,0:T(8,128)(4,1)S(1)} %get-tuple-element.131) | copy-start | bytes 196612
  144.9 18.5 %copy-start.34 = (bf16[128,768]{0,1:T(8,128)(2,1)}, bf16[128,768]{0,1:T(8,128)(2,1)S(1)}, u32[]{:S(2)}) copy-start(bf16[128,768]{0,1:T(8,128)(2,1)S(1)} %copy.108) | copy-start | bytes 589828
  163.4 91.4 %copy-start.9 = (bf16[1,512,768]{1,2,0:T(8,128)(2,1)}, bf16[1,512,768]{1,2,0:T(8,128)(2,1)S(1)}, u32[]{:S(2)}) copy-start(bf16[1,512,768]{1,2,0:T(8,128)(2,1)S(1)} %copy.107) | copy-start | bytes 2359300
  168.2 86.5 %copy-start.30 = (bf16[12,64,128]{2,1,0:T(8,128)(2,1)}, bf16[12,64,128]{2,1,0:T(8,128)(2,1)S(1)}, u32[]{:S(2)}) copy-start(bf16[12,64,128]{2,1,0:T(8,128)(2,1)S(1)} %convolution_convert_fusion.20) | copy-start | bytes 589828
  170.0 114.8 %copy-start.16 = (f32[128,768]{1,0:T(8,128)}, f32[128,768]{1,0:T(8,128)S(1)}, u32[]{:S(2)}) copy-start(f32[128,768]{1,0:T(8,128)S(1)} %get-tuple-element.136) | copy-start | bytes 1179652
  170.6 87.3 %copy-start.82 = (f32[128]{0:T(128)}, f32[128]{0:T(128)S(1)}, u32[]{:S(2)}) copy-start(f32[128]{0:T(128)S(1)} %get-tuple-element.128) | copy-start | bytes 1540
  257.9 8.0 %copy-start.4 = (f32[12,128,512]{2,1,0:T(8,128)}, f32[12,128,512]{2,1,0:T(8,128)S(1)}, u32[]{:S(2)}) copy-start(f32[12,128,512]{2,1,0:T(8,128)S(1)} %get-tuple-element.138) | copy-start | bytes 9437188
  271.7 216.6 %reduce-scatter.7.cloned.1.call-start = ((), (), s32[]{:S(2)}) async-start(), calls=%async_computation.8 | async-start | bytes 4866048 | tf_op jit(solution)/shard_map/reduce_scatter | solution.py:47
  271.9 17.4 %copy-start.15 = (f32[128,768]{1,0:T(8,128)}, f32[128,768]{1,0:T(8,128)S(1)}, u32[]{:S(2)}) copy-start(f32[128,768]{1,0:T(8,128)S(1)} %subtract_add_fusion.1) | copy-start | bytes 1179652
  281.1 10.9 %collective-permute-start.3 = (bf16[1,128,1536]{1,2,0:T(8,128)(2,1)}, bf16[1,128,1536]{1,2,0:T(8,128)(2,1)}, u32[]{:S(2)}, u32[]{:S(2)}) collective-permute-start(bf16[1,128,1536]{1,2,0:T(8,128)(2,1)} %get-tuple-element.104), channel_id=1, source_target_pairs={{0,1},{1,2},{2,3},{3,0},{4,5},{5,6},{6,7},{7,4},{8,9},{9,10},{10,1... | collective-permute-start | bytes 1179656 | tf_op jit(solution)/shard_map/ppermute | solution.py:58
  281.4 12.3 %collective-permute-start.4 = (bf16[1,128,1536]{1,2,0:T(8,128)(2,1)}, bf16[1,128,1536]{1,2,0:T(8,128)(2,1)}, u32[]{:S(2)}, u32[]{:S(2)}) collective-permute-start(bf16[1,128,1536]{1,2,0:T(8,128)(2,1)} %get-tuple-element.105), channel_id=1, source_target_pairs={{0,2},{1,3},{2,0},{3,1},{4,6},{5,7},{6,4},{7,5},{8,10},{9,11},{10,... | collective-permute-start | bytes 1179656 | tf_op jit(solution)/shard_map/ppermute | solution.py:58
  282.9 17.4 %collective-permute-start.5 = (bf16[1,128,1536]{1,2,0:T(8,128)(2,1)}, bf16[1,128,1536]{1,2,0:T(8,128)(2,1)}, u32[]{:S(2)}, u32[]{:S(2)}) collective-permute-start(bf16[1,128,1536]{1,2,0:T(8,128)(2,1)} %get-tuple-element.106), channel_id=1, source_target_pairs={{0,3},{1,0},{2,1},{3,2},{4,7},{5,4},{6,5},{7,6},{8,11},{9,8},{10,9... | collective-permute-start | bytes 1179656 | tf_op jit(solution)/shard_map/ppermute | solution.py:58
  290.8 11.8 %copy-start.17 = (bf16[768,768]{1,0:T(8,128)(2,1)S(1)}, bf16[768,768]{1,0:T(8,128)(2,1)}, u32[]{:S(2)}) copy-start(bf16[768,768]{1,0:T(8,128)(2,1)} %copy.119) | copy-start | bytes 3538948
  305.2 9.2 %copy-start.3 = (f32[12,128,512]{2,1,0:T(8,128)S(1)}, f32[12,128,512]{2,1,0:T(8,128)}, u32[]{:S(2)}) copy-start(f32[12,128,512]{2,1,0:T(8,128)} %copy-done.2) | copy-start | bytes 9437188
  305.2 295.5 %reduce-scatter.5.cloned.1.call-start = ((), (), s32[]{:S(2)}) async-start(), calls=%async_computation.7 | async-start | bytes 4866048 | tf_op jit(solution)/shard_map/reduce_scatter | solution.py:47
  319.6 14.6 %collective-permute-start = (bf16[1,128,1536]{1,2,0:T(8,128)(2,1)S(1)}, bf16[1,128,1536]{1,2,0:T(8,128)(2,1)S(1)}, u32[]{:S(2)}, u32[]{:S(2)}) collective-permute-start(bf16[1,128,1536]{1,2,0:T(8,128)(2,1)S(1)} %get-tuple-element.107), channel_id=1, source_target_pairs={{0,1},{1,2},{2,3},{3,0},{4,5},{5,6},{6,7},{7,4},{8,9},{9,10},{10,1... | collective-permute-start | bytes 1179656 | tf_op jit(solution)/shard_map/ppermute | solution.py:58
  320.6 14.5 %collective-permute-start.1 = (bf16[1,128,1536]{1,2,0:T(8,128)(2,1)S(1)}, bf16[1,128,1536]{1,2,0:T(8,128)(2,1)S(1)}, u32[]{:S(2)}, u32[]{:S(2)}) collective-permute-start(bf16[1,128,1536]{1,2,0:T(8,128)(2,1)S(1)} %get-tuple-element.108), channel_id=1, source_target_pairs={{0,2},{1,3},{2,0},{3,1},{4,6},{5,7},{6,4},{7,5},{8,10},{9,11},{10,... | collective-permute-start | bytes 1179656 | tf_op jit(solution)/shard_map/ppermute | solution.py:58
  322.1 18.9 %collective-permute-start.2 = (bf16[1,128,1536]{1,2,0:T(8,128)(2,1)S(1)}, bf16[1,128,1536]{1,2,0:T(8,128)(2,1)S(1)}, u32[]{:S(2)}, u32[]{:S(2)}) collective-permute-start(bf16[1,128,1536]{1,2,0:T(8,128)(2,1)S(1)} %get-tuple-element.109), channel_id=1, source_target_pairs={{0,3},{1,0},{2,1},{3,2},{4,7},{5,4},{6,5},{7,6},{8,11},{9,8},{10,9... | collective-permute-start | bytes 1179656 | tf_op jit(solution)/shard_map/ppermute | solution.py:58
  322.8 18.4 %copy-start.21 = (bf16[1,128,768]{2,1,0:T(8,128)(2,1)S(1)}, bf16[1,128,768]{2,1,0:T(8,128)(2,1)}, u32[]{:S(2)}) copy-start(bf16[1,128,768]{2,1,0:T(8,128)(2,1)} %param.21) | copy-start | bytes 589828
  322.8 18.4 %copy-start.73 = (f32[768]{0:T(1024)S(1)}, f32[768]{0:T(1024)}, u32[]{:S(2)}) copy-start(f32[768]{0:T(1024)} %copy-done.72) | copy-start | bytes 9220
  322.8 18.4 %copy-start.85 = (f32[128]{0:T(128)S(1)}, f32[128]{0:T(128)}, u32[]{:S(2)}) copy-start(f32[128]{0:T(128)} %copy-done.84) | copy-start | bytes 1540
  323.5 18.9 %copy-start.47 = (bf16[12,64,128]{2,1,0:T(8,128)(2,1)}, bf16[12,64,128]{2,1,0:T(8,128)(2,1)S(1)}, u32[]{:S(2)}) copy-start(bf16[12,64,128]{2,1,0:T(8,128)(2,1)S(1)} %convolution_convert_fusion.14) | copy-start | bytes 589828
  345.3 374.7 %reduce-scatter.9.cloned.1.call-start = ((), (), s32[]{:S(2)}) async-start(), calls=%async_computation.9 | async-start | bytes 6488064 | tf_op jit(solution)/shard_map/reduce_scatter | solution.py:47
  363.7 10.5 %copy-start.8 = (bf16[2048,768]{1,0:T(8,128)(2,1)S(1)}, bf16[2048,768]{1,0:T(8,128)(2,1)}, u32[]{:S(2)}) copy-start(bf16[2048,768]{1,0:T(8,128)(2,1)} %all-gather.10.cloned.1.call-done) | copy-start | bytes 9437188
  369.9 3.0 collective-permute-start.6
  371.9 7.2 copy-start.42
  373.7 10.3 %copy-start.94 = (f32[128]{0:T(128)S(1)}, f32[128]{0:T(128)}, u32[]{:S(2)}) copy-start(f32[128]{0:T(128)} %get-tuple-element.98) | copy-start | bytes 1540
  373.7 14.9 %copy-start.14 = (f32[128,768]{1,0:T(8,128)S(1)}, f32[128,768]{1,0:T(8,128)}, u32[]{:S(2)}) copy-start(f32[128,768]{1,0:T(8,128)} %copy-done.12) | copy-start | bytes 1179652
  373.7 14.9 %copy-start.22 = (bf16[1,128,768]{2,1,0:T(8,128)(2,1)S(1)}, bf16[1,128,768]{2,1,0:T(8,128)(2,1)}, u32[]{:S(2)}) copy-start(bf16[1,128,768]{2,1,0:T(8,128)(2,1)} %param.21) | copy-start | bytes 589828
  373.7 14.9 %copy-start.54 = (f32[128,768]{1,0:T(8,128)S(1)}, f32[128,768]{1,0:T(8,128)}, u32[]{:S(2)}) copy-start(f32[128,768]{1,0:T(8,128)} %get-tuple-element.147) | copy-start | bytes 1179652
  373.7 14.9 %copy-start.74 = (f32[768]{0:T(1024)S(1)}, f32[768]{0:T(1024)}, u32[]{:S(2)}) copy-start(f32[768]{0:T(1024)} %copy-done.72) | copy-start | bytes 9220
  373.7 14.9 %copy-start.86 = (f32[128]{0:T(128)S(1)}, f32[128]{0:T(128)}, u32[]{:S(2)}) copy-start(f32[128]{0:T(128)} %copy-done.84) | copy-start | bytes 1540
  373.8 14.9 %copy-start.87 = (f32[128]{0:T(128)S(1)}, f32[128]{0:T(128)}, u32[]{:S(2)}) copy-start(f32[128]{0:T(128)} %get-tuple-element.125) | copy-start | bytes 1540
  373.8 3.8 collective-permute-start.7
  377.6 5.0 collective-permute-start.8
  379.1 343.3 %copy-start.1 = (bf16[1,512,768]{2,1,0:T(8,128)(2,1)S(1)}, bf16[1,512,768]{2,1,0:T(8,128)(2,1)}, u32[]{:S(2)}) copy-start(bf16[1,512,768]{2,1,0:T(8,128)(2,1)} %param.22) | copy-start | bytes 2359300
  382.5 3.7 collective-permute-start.9
  386.2 4.6 collective-permute-start.10
  (66 other events, 195.6 us)
Sparse Core Ops, SparseCore 0:
  12.3 67.0 all-gather.5
  82.8 57.8 all-gather.9
  142.9 18.4 all-gather.11
  164.2 88.8 all-gather.7
  271.8 105.0 reduce-scatter.10
  382.2 105.9 reduce-scatter.6
  494.6 106.0 reduce-scatter.4
  606.3 113.5 reduce-scatter.8
where the time goes:
time: 735 us; the launch traced here: 729 us
  waiting for transfers between devices  558 us (76%)
  matrix products  74.8 us (10%)
  local copies, waits for them, and re-layouts  42.6 us (6%)
  other arithmetic  24.3 us (3%)
  between operations  15.9 us (2%)
  starting transfers between devices  13.7 us (2%)
    reduce_scatter x4, waiting for transfers between devices, scatter_rows(): lax.psum_scatter(partial, ('fsdp', 'seq'), scatter_dimension=0, tiled=True)  319 us
    all_gather x3, waiting for transfers between devices, gather_rows(): return lax.all_gather(packed, ('fsdp', 'seq'), axis=0, tiled=True)  190 us
    ppermute x6, waiting for transfers between devices, scatter_to_owner(): total = total + lax.ppermute(piece, 'seq', pairs).astype(jnp.float32)  27 us
    dot_general x7, matrix products, times_transposed(): lax.dot_general(first_op, second_op, (((1,), (1,)), ((), ())), preferred_...  22.6 us
    all_gather x1, waiting for transfers between devices, per_device(): lax.all_gather(qkv_one[:, model_width:].reshape(row_count, block_len, 2 *...  16.4 us
  transfers between devices with their start and end apart: 19, of which 17 were waited for; matrix products, arithmetic and copies ran while one was open for 15% of the time, Pallas kernels for 0%

commit v1 on v0

--- a/solution.py
+++ b/solution.py
@@ -8,6 +8,28 @@
 epsilon = 1e-06
 masked_value = -1e30
 highest = lax.Precision.HIGHEST
+
+
+def in_order(parts, dim):
+    shape = list(parts.shape[1:])
+    shape[dim] *= parts.shape[0]
+    return jnp.moveaxis(parts, 0, dim).reshape(shape)
+
+
+def gather_around(x, axis, dim):
+    count = lax.axis_size(axis)
+    pairs = [(i, (i + 1) % count) for i in range(count)]
+    back = [(b, a) for a, b in pairs]
+    lower, upper = ([], [])
+    for hop in range(count - 1):
+        if hop % 2 == 0:
+            lower.append(lax.ppermute(lower[-1] if lower else x, axis, pairs))
+        else:
+            upper.append(lax.ppermute(upper[-1] if upper else x, axis, back))
+    tiles = jnp.stack([*lower[::-1], x, *upper])
+    shift = lax.axis_index(axis) - len(lower)
+    tiles = tiles[(jnp.arange(count) - shift) % count]
+    return in_order(tiles, dim)
 
 
 def matmul(first_op, second_op):
@@ -207,11 +229,8 @@
     norm_one, factor_one = rms_forward(inputs_flat, self_full[0])
     qkv_one = matmul(norm_one, packed_self[:, : 3 * model_width]).astype(jnp.bfloat16)
     query_one = qkv_one[:, :model_width]
-    pair_all = lax.all_gather(
-        qkv_one[:, model_width:].reshape(row_count, block_len, 2 * model_width),
-        "seq",
-        axis=1,
-        tiled=True,
+    pair_all = gather_around(
+        qkv_one[:, model_width:].reshape(row_count, block_len, 2 * model_width), "seq", 1
     )
     key_all = pair_all[:, :, :model_width]
     value_all = pair_all[:, :, model_width:]

time: 735 us -> 714 us (0.971)
  waiting for transfers between devices: 558 us -> 527 us
    all_gather x1 -> x0, waiting for transfers between devices: 16.4 us -> none  [per_device(): lax.all_gather(qkv_one[:, model_width:].reshape(row_count, block_len, 2 *...]
    all_gather x3, waiting for transfers between devices: 190 us -> 175 us  [gather_rows(): return lax.all_gather(packed, ('fsdp', 'seq'), axis=0, tiled=True)]
  transfers between devices with their start and end apart: 19 -> 21, of which waited for: 17 -> 17; matrix products, arithmetic and copies ran while one was open for 15% -> 16% of each run, Pallas kernels for 0% -> 0%
where the time goes in v1:
time: 714 us; the launch traced here: 708 us
  waiting for transfers between devices  527 us (74%)
  matrix products  74.7 us (10%)
  local copies, waits for them, and re-layouts  49.8 us (7%)
  other arithmetic  24.9 us (3%)
  starting transfers between devices  15.8 us (2%)
  between operations  15.7 us (2%)
    reduce_scatter x4, waiting for transfers between devices, scatter_rows(): lax.psum_scatter(partial, ('fsdp', 'seq'), scatter_dimension=0, tiled=True)  319 us
    all_gather x3, waiting for transfers between devices, gather_rows(): return lax.all_gather(packed, ('fsdp', 'seq'), axis=0, tiled=True)  175 us
    ppermute x6, waiting for transfers between devices, scatter_to_owner(): total = total + lax.ppermute(piece, 'seq', pairs).astype(jnp.float32)  27 us
    dot_general x7, matrix products, times_transposed(): lax.dot_general(first_op, second_op, (((1,), (1,)), ((), ())), preferred_...  22.7 us
  transfers between devices with their start and end apart: 21, of which 17 were waited for; matrix products, arithmetic and copies ran while one was open for 16% of the time, Pallas kernels for 0%

profile of v1, /device:TPU:0, one launch (start us, length us, event | category | flops | bytes accessed | tf_op | source)
XLA Modules:
  0.0 707.8 jit_solution(18231951533675399978)
XLA Ops:
  12.3 1.6 reshape.683
  21.2 3.9 fusion.1
  25.1 54.4 %all-gather.4.cloned.1.call-done = bf16[768,3200]{1,0:T(8,128)(2,1)} async-done(((bf16[24,3200]{1,0:T(8,128)(2,1)}), bf16[768,3200]{1,0:T(8,128)(2,1)}) %all-gather.4.cloned.1.call-update) | async-done | bytes 4915216 | tf_op jit(solution)/shard_map/all_gather | solution.py:65
  79.4 2.1 convert_reduce_fusion
  81.6 2.7 convolution_convert_fusion.2
  85.5 5.0 copy.109
  90.7 1.5 collective-permute-start.2
  93.0 47.8 %all-gather.8.cloned.1.call-done = bf16[2048,768]{1,0:T(8,128)(2,1)} async-done(((bf16[64,768]{1,0:T(8,128)(2,1)}), bf16[2048,768]{1,0:T(8,128)(2,1)}) %all-gather.8.cloned.1.call-update) | async-done | bytes 3145744 | tf_op jit(solution)/shard_map/all_gather | solution.py:65
  140.8 4.0 fusion.75
  147.8 1.9 gather_fusion
  149.7 1.5 fusion.97
  151.8 3.1 fusion.99
  156.7 1.8 multiply_reduce_fusion.7
  159.1 72.6 %all-gather.6.cloned.1.call-done = bf16[768,7168]{1,0:T(8,128)(2,1)} async-done(((bf16[24,7168]{1,0:T(8,128)(2,1)}), bf16[768,7168]{1,0:T(8,128)(2,1)}) %all-gather.6.cloned.1.call-update) | async-done | bytes 11010064 | tf_op jit(solution)/shard_map/all_gather | solution.py:65
  231.7 1.6 convolution_convert_fusion.19
  233.5 2.2 convolution_convert_fusion.8
  237.5 2.0 copy-done.23
  244.6 3.0 multiply_reduce_fusion.2
  247.6 2.7 convolution_convert_fusion.4
  250.5 2.0 convolution_convert_fusion.17
  252.7 3.6 multiply_reduce_fusion.1
  264.0 1.6 convolution_convert_fusion.5
  265.6 2.4 copy.117
  270.6 1.6 collective-permute-done.7
  272.3 6.6 collective-permute-done.8
  281.2 2.6 pad_maximum_fusion.1
  283.8 2.8 multiply_reduce_fusion.3
  288.7 2.5 convolution_convert_fusion.15
  291.2 1.7 copy.112
  292.9 2.3 multiply_reduce_fusion
  302.1 10.8 %collective-permute-done.3 = bf16[1,128,1536]{1,2,0:T(8,128)(2,1)S(1)} collective-permute-done((bf16[1,128,1536]{1,2,0:T(8,128)(2,1)S(1)}, bf16[1,128,1536]{1,2,0:T(8,128)(2,1)S(1)}, u32[]{:S(2)}, u32[]{:S(2)}) %collective-permute-start.3) | collective-permute-done | bytes 393248 | tf_op jit(solution)/shard_map/ppermute | solution.py:80
  313.7 5.9 collective-permute-done.5
  321.0 2.8 pad_maximum_fusion
  325.2 4.4 convolution_convert_fusion
  329.6 1.9 copy-done.7
  331.5 3.5 copy.113
  335.0 6.5 fusion.29
  342.3 5.0 fusion.61
  348.5 2.0 collective-permute-start.9
  352.7 2.3 fusion.28
  356.1 1.5 collective-permute-start.11
  357.7 3.4 fusion.22
  362.6 2.2 collective-permute-done.12
  364.8 2.4 collective-permute-start.13
  370.8 1.7 reshape.713
  372.5 94.4 %reduce-scatter.7.cloned.1.call-done = bf16[24,3072]{1,0:T(8,128)(2,1)} async-done(((bf16[768,3072]{1,0:T(8,128)(2,1)}), bf16[24,3072]{1,0:T(8,128)(2,1)}) %reduce-scatter.7.cloned.1.call-update) | async-done | bytes 147472 | tf_op jit(solution)/shard_map/reduce_scatter | solution.py:69
  470.2 109.0 %reduce-scatter.5.cloned.1.call-done = bf16[24,3072]{1,0:T(8,128)(2,1)} async-done(((bf16[768,3072]{1,0:T(8,128)(2,1)}), bf16[24,3072]{1,0:T(8,128)(2,1)}) %reduce-scatter.5.cloned.1.call-update) | async-done | bytes 147472 | tf_op jit(solution)/shard_map/reduce_scatter | solution.py:69
  582.6 115.7 %reduce-scatter.9.cloned.1.call-done = bf16[24,4096]{1,0:T(8,128)(2,1)} async-done(((bf16[768,4096]{1,0:T(8,128)(2,1)}), bf16[24,4096]{1,0:T(8,128)(2,1)}) %reduce-scatter.9.cloned.1.call-update) | async-done | bytes 196624 | tf_op jit(solution)/shard_map/reduce_scatter | solution.py:69
  (313 shorter events, 71.5 us)
Async XLA Ops:
  7.2 226.3 %copy-start = (bf16[1,512,768]{2,1,0:T(8,128)(2,1)S(1)}, bf16[1,512,768]{2,1,0:T(8,128)(2,1)}, u32[]{:S(2)}) copy-start(bf16[1,512,768]{2,1,0:T(8,128)(2,1)} %param.22) | copy-start | bytes 2359300
  7.2 13.3 %copy-start.20 = (bf16[1,128,768]{2,1,0:T(8,128)(2,1)S(1)}, bf16[1,128,768]{2,1,0:T(8,128)(2,1)}, u32[]{:S(2)}) copy-start(bf16[1,128,768]{2,1,0:T(8,128)(2,1)} %param.21) | copy-start | bytes 589828
  7.2 14.0 %copy-start.88 = (bf16[32,12]{0,1:T(8,128)(2,1)S(1)}, bf16[32,12]{0,1:T(8,128)(2,1)}, u32[]{:S(2)}) copy-start(bf16[32,12]{0,1:T(8,128)(2,1)} %param.31) | copy-start | bytes 2308
  7.2 72.2 %all-gather.4.cloned.1.call-start = ((), (), s32[]{:S(2)}) async-start(), calls=%async_computation.4 | async-start | bytes 5068800 | tf_op jit(solution)/shard_map/all_gather | solution.py:65
  12.2 128.6 %all-gather.8.cloned.1.call-start = ((), (), s32[]{:S(2)}) async-start(), calls=%async_computation.6 | async-start | bytes 3244032 | tf_op jit(solution)/shard_map/all_gather | solution.py:65
  14.0 217.7 %all-gather.6.cloned.1.call-start = ((), (), s32[]{:S(2)}) async-start(), calls=%async_computation.5 | async-start | bytes 11354112 | tf_op jit(solution)/shard_map/all_gather | solution.py:65
  20.1 350.7 %reduce-scatter.11.cloned.1.call-start = ((), (), s32[]{:S(2)}) async-start(), calls=%async_computation.10 | async-start | bytes 3244032 | tf_op jit(solution)/shard_map/reduce_scatter | solution.py:69
  20.4 61.2 %copy-start.56 = (s32[128,512]{0,1:T(8,128)}, s32[128,512]{0,1:T(8,128)S(1)}, u32[]{:S(2)}) copy-start(s32[128,512]{0,1:T(8,128)S(1)} %copy.108) | copy-start | bytes 786436
  20.5 61.1 %copy-start.84 = (s32[32]{0:T(128)}, s32[32]{0:T(128)S(1)}, u32[]{:S(2)}) copy-start(s32[32]{0:T(128)S(1)} %get-tuple-element.99) | copy-start | bytes 388
  20.5 61.1 %copy-start.86 = (s32[32]{0:T(128)}, s32[32]{0:T(128)S(1)}, u32[]{:S(2)}) copy-start(s32[32]{0:T(128)S(1)} %get-tuple-element.100) | copy-start | bytes 388
  21.2 60.4 %copy-start.79 = (f32[128]{0:T(128)}, f32[128]{0:T(128)S(1)}, u32[]{:S(2)}) copy-start(f32[128]{0:T(128)S(1)} %get-tuple-element.128) | copy-start | bytes 1540
  81.6 150.1 %copy-start.58 = (f32[768]{0:T(1024)}, f32[768]{0:T(1024)S(1)}, u32[]{:S(2)}) copy-start(f32[768]{0:T(1024)S(1)} %get-tuple-element.91) | copy-start | bytes 9220
  85.1 7.4 %collective-permute-start = (bf16[1,128,1536]{2,1,0:T(8,128)(2,1)}, bf16[1,128,1536]{2,1,0:T(8,128)(2,1)S(1)}, u32[]{:S(2)}, u32[]{:S(2)}) collective-permute-start(bf16[1,128,1536]{2,1,0:T(8,128)(2,1)} %get-tuple-element.113), channel_id=1, source_target_pairs={{0,1},{1,2},{2,3},{3,0},{4,5},{5,6},{6,7},{7,4},{8,9},{9,10},{10,1... | collective-permute-start | bytes 1179656 | tf_op jit(solution)/shard_map/ppermute | solution.py:26
  85.4 55.4 %copy-start.38 = (bf16[1,128,768]{2,1,0:T(8,128)(2,1)S(1)}, bf16[1,128,768]{2,1,0:T(8,128)(2,1)}, u32[]{:S(2)}) copy-start(bf16[1,128,768]{2,1,0:T(8,128)(2,1)} %param.41) | copy-start | bytes 589828
  90.7 149.7 %copy-start.24 = (pred[128,512]{1,0:T(8,128)(4,1)}, pred[128,512]{1,0:T(8,128)(4,1)S(1)}, u32[]{:S(2)}) copy-start(pred[128,512]{1,0:T(8,128)(4,1)S(1)} %get-tuple-element.133) | copy-start | bytes 196612
  90.7 55.0 %collective-permute-start.2 = (bf16[1,128,1536]{2,1,0:T(8,128)(2,1)}, bf16[1,128,1536]{2,1,0:T(8,128)(2,1)S(1)}, u32[]{:S(2)}, u32[]{:S(2)}) collective-permute-start(bf16[1,128,1536]{2,1,0:T(8,128)(2,1)} %get-tuple-element.113), channel_id=1, source_target_pairs={{1,0},{2,1},{3,2},{0,3},{5,4},{6,5},{7,6},{4,7},{9,8},{10,9},{11,1... | collective-permute-start | bytes 1179656 | tf_op jit(solution)/shard_map/ppermute | solution.py:28
  92.5 53.1 %copy-start.53 = (bf16[1,128,1536]{2,1,0:T(8,128)(2,1)}, bf16[1,128,1536]{2,1,0:T(8,128)(2,1)S(1)}, u32[]{:S(2)}) copy-start(bf16[1,128,1536]{2,1,0:T(8,128)(2,1)S(1)} %collective-permute-done) | copy-start | bytes 1179652
  92.5 53.1 %collective-permute-start.1 = (bf16[1,128,1536]{2,1,0:T(8,128)(2,1)S(1)}, bf16[1,128,1536]{2,1,0:T(8,128)(2,1)}, u32[]{:S(2)}, u32[]{:S(2)}) collective-permute-start(bf16[1,128,1536]{2,1,0:T(8,128)(2,1)S(1)} %collective-permute-done), channel_id=1, source_target_pairs={{0,1},{1,2},{2,3},{3,0},{4,5},{5,6},{6,7},{7,4},{8,9},{9,10},{10,1... | collective-permute-start | bytes 1179656 | tf_op jit(solution)/shard_map/ppermute | solution.py:26
  151.8 81.7 %copy-start.9 = (bf16[1,512,768]{1,2,0:T(8,128)(2,1)}, bf16[1,512,768]{1,2,0:T(8,128)(2,1)S(1)}, u32[]{:S(2)}) copy-start(bf16[1,512,768]{1,2,0:T(8,128)(2,1)S(1)} %copy.105) | copy-start | bytes 2359300
  156.7 76.6 %copy-start.30 = (bf16[12,64,128]{2,1,0:T(8,128)(2,1)}, bf16[12,64,128]{2,1,0:T(8,128)(2,1)S(1)}, u32[]{:S(2)}) copy-start(bf16[12,64,128]{2,1,0:T(8,128)(2,1)S(1)} %convolution_convert_fusion.20) | copy-start | bytes 589828
  158.5 104.9 %copy-start.16 = (f32[128,768]{1,0:T(8,128)}, f32[128,768]{1,0:T(8,128)S(1)}, u32[]{:S(2)}) copy-start(f32[128,768]{1,0:T(8,128)S(1)} %get-tuple-element.138) | copy-start | bytes 1179652
  159.1 77.5 %copy-start.77 = (f32[128]{0:T(128)}, f32[128]{0:T(128)S(1)}, u32[]{:S(2)}) copy-start(f32[128]{0:T(128)S(1)} %get-tuple-element.130) | copy-start | bytes 1540
  250.3 216.5 %reduce-scatter.7.cloned.1.call-start = ((), (), s32[]{:S(2)}) async-start(), calls=%async_computation.8 | async-start | bytes 4866048 | tf_op jit(solution)/shard_map/reduce_scatter | solution.py:69
  250.5 17.5 %copy-start.15 = (f32[128,768]{1,0:T(8,128)}, f32[128,768]{1,0:T(8,128)S(1)}, u32[]{:S(2)}) copy-start(f32[128,768]{1,0:T(8,128)S(1)} %subtract_add_fusion.1) | copy-start | bytes 1179652
  259.7 10.9 %collective-permute-start.6 = (bf16[1,128,1536]{1,2,0:T(8,128)(2,1)}, bf16[1,128,1536]{1,2,0:T(8,128)(2,1)}, u32[]{:S(2)}, u32[]{:S(2)}) collective-permute-start(bf16[1,128,1536]{1,2,0:T(8,128)(2,1)} %get-tuple-element.104), channel_id=1, source_target_pairs={{0,1},{1,2},{2,3},{3,0},{4,5},{5,6},{6,7},{7,4},{8,9},{9,10},{10,1... | collective-permute-start | bytes 1179656 | tf_op jit(solution)/shard_map/ppermute | solution.py:80
  260.0 12.3 %collective-permute-start.7 = (bf16[1,128,1536]{1,2,0:T(8,128)(2,1)}, bf16[1,128,1536]{1,2,0:T(8,128)(2,1)}, u32[]{:S(2)}, u32[]{:S(2)}) collective-permute-start(bf16[1,128,1536]{1,2,0:T(8,128)(2,1)} %get-tuple-element.105), channel_id=1, source_target_pairs={{0,2},{1,3},{2,0},{3,1},{4,6},{5,7},{6,4},{7,5},{8,10},{9,11},{10,... | collective-permute-start | bytes 1179656 | tf_op jit(solution)/shard_map/ppermute | solution.py:80
  261.5 17.4 %collective-permute-start.8 = (bf16[1,128,1536]{1,2,0:T(8,128)(2,1)}, bf16[1,128,1536]{1,2,0:T(8,128)(2,1)}, u32[]{:S(2)}, u32[]{:S(2)}) collective-permute-start(bf16[1,128,1536]{1,2,0:T(8,128)(2,1)} %get-tuple-element.106), channel_id=1, source_target_pairs={{0,3},{1,0},{2,1},{3,2},{4,7},{5,4},{6,5},{7,6},{8,11},{9,8},{10,9... | collective-permute-start | bytes 1179656 | tf_op jit(solution)/shard_map/ppermute | solution.py:80
  283.8 295.4 %reduce-scatter.5.cloned.1.call-start = ((), (), s32[]{:S(2)}) async-start(), calls=%async_computation.7 | async-start | bytes 4866048 | tf_op jit(solution)/shard_map/reduce_scatter | solution.py:69
  298.3 14.6 %collective-permute-start.3 = (bf16[1,128,1536]{1,2,0:T(8,128)(2,1)S(1)}, bf16[1,128,1536]{1,2,0:T(8,128)(2,1)S(1)}, u32[]{:S(2)}, u32[]{:S(2)}) collective-permute-start(bf16[1,128,1536]{1,2,0:T(8,128)(2,1)S(1)} %get-tuple-element.107), channel_id=1, source_target_pairs={{0,1},{1,2},{2,3},{3,0},{4,5},{5,6},{6,7},{7,4},{8,9},{9,10},{10,1... | collective-permute-start | bytes 1179656 | tf_op jit(solution)/shard_map/ppermute | solution.py:80
  299.2 14.5 %collective-permute-start.4 = (bf16[1,128,1536]{1,2,0:T(8,128)(2,1)S(1)}, bf16[1,128,1536]{1,2,0:T(8,128)(2,1)S(1)}, u32[]{:S(2)}, u32[]{:S(2)}) collective-permute-start(bf16[1,128,1536]{1,2,0:T(8,128)(2,1)S(1)} %get-tuple-element.108), channel_id=1, source_target_pairs={{0,2},{1,3},{2,0},{3,1},{4,6},{5,7},{6,4},{7,5},{8,10},{9,11},{10,... | collective-permute-start | bytes 1179656 | tf_op jit(solution)/shard_map/ppermute | solution.py:80
  300.7 18.9 %collective-permute-start.5 = (bf16[1,128,1536]{1,2,0:T(8,128)(2,1)S(1)}, bf16[1,128,1536]{1,2,0:T(8,128)(2,1)S(1)}, u32[]{:S(2)}, u32[]{:S(2)}) collective-permute-start(bf16[1,128,1536]{1,2,0:T(8,128)(2,1)S(1)} %get-tuple-element.109), channel_id=1, source_target_pairs={{0,3},{1,0},{2,1},{3,2},{4,7},{5,4},{6,5},{7,6},{8,11},{9,8},{10,9... | collective-permute-start | bytes 1179656 | tf_op jit(solution)/shard_map/ppermute | solution.py:80
  301.4 18.4 %copy-start.21 = (bf16[1,128,768]{2,1,0:T(8,128)(2,1)S(1)}, bf16[1,128,768]{2,1,0:T(8,128)(2,1)}, u32[]{:S(2)}) copy-start(bf16[1,128,768]{2,1,0:T(8,128)(2,1)} %param.21) | copy-start | bytes 589828
  301.4 18.4 %copy-start.68 = (f32[768]{0:T(1024)S(1)}, f32[768]{0:T(1024)}, u32[]{:S(2)}) copy-start(f32[768]{0:T(1024)} %copy-done.67) | copy-start | bytes 9220
  301.4 18.4 %copy-start.80 = (f32[128]{0:T(128)S(1)}, f32[128]{0:T(128)}, u32[]{:S(2)}) copy-start(f32[128]{0:T(128)} %copy-done.79) | copy-start | bytes 1540
  302.1 18.9 %copy-start.46 = (bf16[12,64,128]{2,1,0:T(8,128)(2,1)}, bf16[12,64,128]{2,1,0:T(8,128)(2,1)S(1)}, u32[]{:S(2)}) copy-start(bf16[12,64,128]{2,1,0:T(8,128)(2,1)S(1)} %convolution_convert_fusion.14) | copy-start | bytes 589828
  323.9 374.4 %reduce-scatter.9.cloned.1.call-start = ((), (), s32[]{:S(2)}) async-start(), calls=%async_computation.9 | async-start | bytes 6488064 | tf_op jit(solution)/shard_map/reduce_scatter | solution.py:69
  348.5 3.0 collective-permute-start.9
  352.3 14.9 %copy-start.14 = (f32[128,768]{1,0:T(8,128)S(1)}, f32[128,768]{1,0:T(8,128)}, u32[]{:S(2)}) copy-start(f32[128,768]{1,0:T(8,128)} %copy-done.12) | copy-start | bytes 1179652
  352.3 14.9 %copy-start.22 = (bf16[1,128,768]{2,1,0:T(8,128)(2,1)S(1)}, bf16[1,128,768]{2,1,0:T(8,128)(2,1)}, u32[]{:S(2)}) copy-start(bf16[1,128,768]{2,1,0:T(8,128)(2,1)} %param.21) | copy-start | bytes 589828
  352.3 14.9 %copy-start.55 = (f32[128,768]{1,0:T(8,128)S(1)}, f32[128,768]{1,0:T(8,128)}, u32[]{:S(2)}) copy-start(f32[128,768]{1,0:T(8,128)} %get-tuple-element.149) | copy-start | bytes 1179652
  352.3 14.9 %copy-start.69 = (f32[768]{0:T(1024)S(1)}, f32[768]{0:T(1024)}, u32[]{:S(2)}) copy-start(f32[768]{0:T(1024)} %copy-done.67) | copy-start | bytes 9220
  352.3 14.9 %copy-start.81 = (f32[128]{0:T(128)S(1)}, f32[128]{0:T(128)}, u32[]{:S(2)}) copy-start(f32[128]{0:T(128)} %copy-done.79) | copy-start | bytes 1540
  352.3 14.9 %copy-start.82 = (f32[128]{0:T(128)S(1)}, f32[128]{0:T(128)}, u32[]{:S(2)}) copy-start(f32[128]{0:T(128)} %get-tuple-element.127) | copy-start | bytes 1540
  352.4 3.8 collective-permute-start.10
  356.1 5.0 collective-permute-start.11
  357.7 343.0 %copy-start.1 = (bf16[1,512,768]{2,1,0:T(8,128)(2,1)S(1)}, bf16[1,512,768]{2,1,0:T(8,128)(2,1)}, u32[]{:S(2)}) copy-start(bf16[1,512,768]{2,1,0:T(8,128)(2,1)} %param.22) | copy-start | bytes 2359300
  361.1 3.7 collective-permute-start.12
  364.8 4.6 collective-permute-start.13
  (63 other events, 232.9 us)
Sparse Core Ops, SparseCore 0:
  12.4 67.0 all-gather.3
  82.9 57.8 all-gather.7
  143.7 87.9 all-gather.5
  250.4 105.0 reduce-scatter.10
  360.8 105.9 reduce-scatter.6
  473.0 106.0 reduce-scatter.4
  584.8 113.4 reduce-scatter.8
